TPU v7x, 128 devices: a whole 4x4x4 slice. The times are simulated.
128 devices in a mesh: bucket: 8 (over z, y_lo), dom: 16 (over y_hi, x, core).
Axes of the slice: x: 4, y: 4 (y_hi: 2, y_lo: 2; y = y_hi * 2 + y_lo), z: 4, core: 2. Of those that a mesh axis runs over, the one named last changes fastest.
Arguments:
- entity_table: float32 [16, 512, 400], P('bucket', 'dom'), may hold values from -3 to 3
- adagrad_state: float32 [16, 512], P('bucket', 'dom'), may hold values from 0.1 to 10
- relations: float32 [7424, 400], replicated, may hold values from -3 to 3
- roster: int32 [4, 8, 2], replicated, may hold values from 0 to 15, as said below
- edge_triples: int32 [128, 128, 4, 8, 3], P(('bucket', 'dom')), may hold values from 0 to 8191, as said below
- counts: int32 [128, 128, 4], P(('bucket', 'dom')), may hold values from 0 to 8, as said below
- negatives: int32 [4, 8, 16, 16, 512], P(None, 'bucket', 'dom'), may hold values from 0 to 511
Outputs:
- updated_table: float32 [16, 512, 400], P('bucket', 'dom')
- updated_state: float32 [16, 512], P('bucket', 'dom')
Inputs may be any that keep to these rules, and one draw needn't show every extreme that they name: In each step every partition 0 to 15 appears exactly once in roster[s]. `edge_triples`: for receiving device w * 16 + j and step s, every head lies in partition roster[s, w, 0] and every tail in partition roster[s, w, 1]; relation ids lie in 0 to 7423, entity ids in 0 to 8191. `counts`: in every step some receiving device gets 8 live slots from every sending device.
All inputs are finite; a program needn't handle non-finite values.
Results may differ from a plain program's by a relative error of at most 0.0003.
Values sent between devices are 32-bit elements; how exact they have to be, the bound alone decides.
No kernel may reach another device: no remote copies, remote signals or barrier semaphores. Data moves between devices by JAX's collectives and lax.ppermute only.
A program may use at most 128 MiB of HBM per device.

v0:
```python
import jax
import jax.numpy as jnp
from jax import lax
from jax.sharding import PartitionSpec as P

cubic_weight = 0.1
learn_rate = 0.05
epsilon = 1e-06


def rotate(left, right):
    half = left.shape[1] // 2
    left_re, left_im = (left[:, :half], left[:, half:])
    right_re, right_im = (right[:, :half], right[:, half:])
    return jnp.concatenate(
        [left_re * right_re - left_im * right_im, left_re * right_im + left_im * right_re], axis=1
    )


def unrotate(grad, right):
    half = grad.shape[1] // 2
    grad_re, grad_im = (grad[:, :half], grad[:, half:])
    right_re, right_im = (right[:, :half], right[:, half:])
    return jnp.concatenate(
        [grad_re * right_re + grad_im * right_im, grad_im * right_re - grad_re * right_im], axis=1
    )


def cubic_grad(values):
    half = values.shape[1] // 2
    real_part, imag_part = (values[:, :half], values[:, half:])
    modulus = jnp.sqrt(real_part * real_part + imag_part * imag_part)
    return 3.0 * cubic_weight * jnp.concatenate([modulus * real_part, modulus * imag_part], axis=1)


def contract_rows(left, right):
    return lax.dot_general(left, right, (((0,), (0,)), ((), ())), precision=lax.Precision.HIGHEST)


def slot_terms(part_src, part_dst, relations, triples, valid, negs, src_label, dst_label):
    prows = part_src.shape[0]
    head_local = triples[:, 0] - src_label * prows
    tail_local = triples[:, 2] - dst_label * prows
    head_rows = jnp.take(part_src, head_local, axis=0)
    rel_rows = jnp.take(relations, triples[:, 1], axis=0)
    tail_rows = jnp.take(part_dst, tail_local, axis=0)
    query = rotate(head_rows, rel_rows)
    scores = lax.dot_general(
        query, part_dst, (((1,), (1,)), ((), ())), precision=lax.Precision.HIGHEST
    )
    column = jnp.arange(prows, dtype=jnp.int32)
    head_hot = (head_local[:, None] == column[None, :]).astype(jnp.float32)
    tail_hot = (tail_local[:, None] == column[None, :]).astype(jnp.float32)
    nblock = negs.shape[0]
    block_counts = jnp.sum((negs[:, :, None] == column[None, None, :]).astype(jnp.float32), axis=1)
    weight = (block_counts[:, None, :] + tail_hot.reshape(nblock, -1, prows)).reshape(scores.shape)
    live = weight > 0
    top = jnp.max(jnp.where(live, scores, -1e30), axis=1, keepdims=True)
    terms = weight * jnp.exp(jnp.where(live, scores - top, -1e30))
    total = jnp.sum(terms, axis=1, keepdims=True)
    adjoint = valid[:, None] * (terms / total - tail_hot)
    grad_query = jnp.dot(adjoint, part_dst, precision=lax.Precision.HIGHEST)
    head_total = unrotate(grad_query, rel_rows) + valid[:, None] * cubic_grad(head_rows)
    tail_reg = valid[:, None] * cubic_grad(tail_rows)
    return (head_hot, tail_hot, adjoint, query, head_total, tail_reg)


def adagrad(values, state, grad):
    new_state = state + jnp.mean(grad * grad, axis=-1)
    return (values - learn_rate * grad / jnp.sqrt(new_state + epsilon)[..., None], new_state)


def select_fold(labels_all, wanted, pieces):
    flat_labels = labels_all.reshape(-1)
    piece_rows, piece_state = pieces
    matches = wanted[:, None] == flat_labels[None, :]
    rows_sum = jnp.sum(jnp.where(matches[:, :, None, None], piece_rows[None], 0.0), axis=1)
    state_sum = jnp.sum(jnp.where(matches[:, :, None], piece_state[None], 0.0), axis=1)
    return (rows_sum, state_sum)


def fetch_rows(rows_held, state_held, labels_all, wanted):
    return select_fold(
        labels_all,
        wanted,
        (
            lax.all_gather(rows_held, "bucket", axis=0, tiled=True),
            lax.all_gather(state_held, "bucket", axis=0, tiled=True),
        ),
    )


def send_home(rows_held, state_held, labels_all, wanted):
    return select_fold(
        labels_all,
        wanted,
        (
            lax.all_gather(rows_held, "bucket", axis=0, tiled=True),
            lax.all_gather(state_held, "bucket", axis=0, tiled=True),
        ),
    )


def local(entity_table, adagrad_state, relations, roster, edge_triples, counts, negatives):
    buckets = lax.axis_size("bucket")
    my_bucket = lax.axis_index("bucket")
    steps = edge_triples.shape[2]
    cap = edge_triples.shape[3]
    edge_in, count_in = (
        lax.all_to_all(edge_triples[0], ("bucket", "dom"), split_axis=0, concat_axis=0, tiled=True),
        lax.all_to_all(counts[0], ("bucket", "dom"), split_axis=0, concat_axis=0, tiled=True),
    )
    owner_labels = jnp.arange(2 * buckets, dtype=jnp.int32).reshape(buckets, 2)
    home_labels = 2 * my_bucket + jnp.arange(2, dtype=jnp.int32)
    rows_held, state_held = (entity_table, adagrad_state)
    for step_index in range(steps):
        wanted = roster[step_index, my_bucket]
        mine_rows, mine_state = fetch_rows(rows_held, state_held, owner_labels, wanted)
        full_rows = lax.all_gather(mine_rows, "dom", axis=1, tiled=True)
        triples = edge_in[:, step_index].reshape(-1, 3)
        slot_live = (
            (jnp.arange(cap, dtype=jnp.int32)[None, :] < count_in[:, step_index][:, None])
            .astype(jnp.float32)
            .reshape(-1)
        )
        head_hot, tail_hot, adjoint, query, head_total, tail_reg = slot_terms(
            full_rows[0],
            full_rows[1],
            relations,
            triples,
            slot_live,
            negatives[step_index, 0, 0],
            wanted[0],
            wanted[1],
        )
        src_side = contract_rows(head_hot, head_total)
        dst_side = contract_rows(adjoint, query) + contract_rows(tail_hot, tail_reg)
        shares = lax.psum_scatter(
            jnp.concatenate([src_side, dst_side], axis=1), "dom", scatter_dimension=0, tiled=True
        )
        width = mine_rows.shape[2]
        grads = jnp.stack([shares[:, :width], shares[:, width:]])
        new_rows, new_state = adagrad(mine_rows, mine_state, grads)
        rows_held, state_held = send_home(new_rows, new_state, roster[step_index], home_labels)
    return (rows_held, state_held)


def solution(mesh):
    in_specs = (
        P("bucket", "dom", None),
        P("bucket", "dom"),
        P(),
        P(),
        P(("bucket", "dom"), None, None, None, None),
        P(("bucket", "dom"), None, None),
        P(None, "bucket", "dom", None, None),
    )
    out_specs = (P("bucket", "dom", None), P("bucket", "dom"))
    return jax.shard_map(local, mesh=mesh, in_specs=in_specs, out_specs=out_specs, check_vma=False)
```

profile of v0, /device:TPU:2, one launch (start us, length us, event | category | flops | bytes accessed | tf_op | source)
XLA Modules:
  0.0 983.3 jit_solution(17356970910296015559)
XLA Ops:
  7.2 34.7 %all_gather.60 = f32[16,32,400]{2,1,0:T(8,128)S(1)} all-gather(f32[2,32,400]{2,1,0:T(8,128)} %param.11), channel_id=1, replica_groups=mesh['bucket'=8,'dom'=16] {'bucket'}, dimensions={0}, use_global_device_ids=true | all-gather | bytes 921600 | tf_op jit(solution)/shard_map/all_gather | solution.py:87
  45.9 8.8 all-to-all-start.1
  55.3 4.7 convert_reduce_fusion.2
  63.0 14.1 %copy.266 = f32[7424,400]{1,0:T(8,128)} copy(f32[7424,400]{0,1:T(8,128)} %param.13) | data formatting | bytes 23756800 | tf_op args[2]
  79.3 9.8 all-to-all-start
  90.3 14.7 %all-to-all-done = s32[128,4,8,3]{2,1,3,0:T(4,128)S(1)} async-done(((s32[128,4,8,3]{2,1,3,0:T(4,128)}), s32[128,4,8,3]{2,1,3,0:T(4,128)S(1)}, u32[]{:S(2)}, u32[]{:S(2)}) %all-to-all-start) | async-done | bytes 49184 | tf_op jit(solution)/shard_map/all_to_all | solution.py:110
  106.5 9.3 gather_fusion.1
  118.2 2.8 broadcast_select_fusion.10
  121.0 4.0 fusion.147
  126.1 4.9 gather_fusion
  130.9 2.9 copy.265
  138.2 3.9 select_reduce_fusion.10
  142.9 4.2 fusion.46
  147.1 4.4 fusion.94
  151.5 4.9 gather_fusion.2
  167.9 15.3 %all-gather = f32[8,2,32]{2,1,0:T(2,128)S(1)} all-gather(f32[1,2,32]{2,1,0:T(2,128)S(1)} %bitcast.199), channel_id=1, replica_groups=mesh['bucket'=8,'dom'=16] {'bucket'}, dimensions={0}, use_global_device_ids=true | all-gather | bytes 2304 | tf_op jit(solution)/shard_map/all_gather | solution.py:88
  184.0 49.1 %reduce-scatter.13.cloned.1.call-done = f32[32,800]{1,0:T(8,128)} async-done(((f32[512,800]{1,0:T(8,128)}), f32[32,800]{1,0:T(8,128)}) %reduce-scatter.13.cloned.1.call-update) | async-done | bytes 102416 | tf_op jit(solution)/shard_map/reduce_scatter | solution.py:138
  234.9 33.0 %all_gather.63 = f32[16,32,400]{2,1,0:T(8,128)S(1)} all-gather(f32[2,32,400]{2,1,0:T(8,128)S(1)} %divide_subtract_fusion.3), channel_id=1, replica_groups=mesh['bucket'=8,'dom'=16] {'bucket'}, dimensions={0}, use_global_device_ids=true | all-gather | bytes 921600 | tf_op jit(solution)/shard_map/all_gather | solution.py:98
  268.1 32.0 %all_gather.64 = f32[16,32,400]{2,1,0:T(8,128)S(1)} all-gather(f32[2,32,400]{2,1,0:T(8,128)S(1)} %select_reduce_fusion.9), channel_id=1, replica_groups=mesh['bucket'=8,'dom'=16] {'bucket'}, dimensions={0}, use_global_device_ids=true | all-gather | bytes 921600 | tf_op jit(solution)/shard_map/all_gather | solution.py:87
  306.6 10.8 %gather_fusion.4 = f32[1024,400]{1,0:T(8,128)} fusion(f32[7424,400]{1,0:T(8,128)} %copy.266, s32[1024]{0:T(1024)S(1)} %fusion.108), kind=kCustom, calls=%fused_computation.9.clone | custom fusion | bytes 3280896 | tf_op jit(solution)/shard_map/jit(_take)/gather | solution.py:45
  320.2 2.8 broadcast_select_fusion.7
  323.0 25.1 %all-gather.15.cloned.1.call-done = f32[2,512,400]{2,0,1:T(2,128)} async-done(((f32[2,32,400]{2,0,1:T(2,128)}), f32[2,512,400]{2,0,1:T(2,128)}) %all-gather.15.cloned.1.call-update) | async-done | bytes 1638416 | tf_op jit(solution)/shard_map/all_gather | solution.py:119
  348.0 5.0 fusion.146
  353.1 4.9 gather_fusion.3
  358.0 3.1 copy.276
  366.1 3.8 select_reduce_fusion.7
  370.6 4.2 fusion.44
  374.8 4.4 fusion.91
  379.2 3.5 gather_fusion.5
  394.8 18.1 %all-gather.1 = f32[8,2,32]{2,1,0:T(2,128)S(1)} all-gather(f32[1,2,32]{2,1,0:T(2,128)S(1)} %copy-done.42), channel_id=1, replica_groups=mesh['bucket'=8,'dom'=16] {'bucket'}, dimensions={0}, use_global_device_ids=true | all-gather | bytes 2304 | tf_op jit(solution)/shard_map/all_gather | solution.py:99
  412.9 15.1 %all-gather.2 = f32[8,2,32]{2,1,0:T(2,128)S(1)} all-gather(f32[1,2,32]{2,1,0:T(2,128)S(1)} %bitcast.196), channel_id=1, replica_groups=mesh['bucket'=8,'dom'=16] {'bucket'}, dimensions={0}, use_global_device_ids=true | all-gather | bytes 2304 | tf_op jit(solution)/shard_map/all_gather | solution.py:88
  428.1 35.2 %reduce-scatter.15.cloned.1.call-done = f32[32,800]{1,0:T(8,128)} async-done(((f32[512,800]{1,0:T(8,128)}), f32[32,800]{1,0:T(8,128)}) %reduce-scatter.15.cloned.1.call-update) | async-done | bytes 102416 | tf_op jit(solution)/shard_map/reduce_scatter | solution.py:138
  464.6 32.9 %all_gather.68 = f32[16,32,400]{2,1,0:T(8,128)S(1)} all-gather(f32[2,32,400]{2,1,0:T(8,128)S(1)} %divide_subtract_fusion.2), channel_id=1, replica_groups=mesh['bucket'=8,'dom'=16] {'bucket'}, dimensions={0}, use_global_device_ids=true | all-gather | bytes 921600 | tf_op jit(solution)/shard_map/all_gather | solution.py:98
  497.8 31.9 %all_gather.69 = f32[16,32,400]{2,1,0:T(8,128)S(1)} all-gather(f32[2,32,400]{2,1,0:T(8,128)S(1)} %select_reduce_fusion.6), channel_id=1, replica_groups=mesh['bucket'=8,'dom'=16] {'bucket'}, dimensions={0}, use_global_device_ids=true | all-gather | bytes 921600 | tf_op jit(solution)/shard_map/all_gather | solution.py:87
  532.6 4.7 convert_reduce_fusion
  541.5 10.6 %gather_fusion.7 = f32[1024,400]{1,0:T(8,128)} fusion(f32[7424,400]{1,0:T(8,128)} %copy.266, s32[1024]{0:T(1024)S(1)} %fusion.111), kind=kCustom, calls=%fused_computation.10.clone | custom fusion | bytes 3280896 | tf_op jit(solution)/shard_map/jit(_take)/gather | solution.py:45
  555.0 2.8 broadcast_select_fusion.4
  557.8 20.0 %all-gather.17.cloned.1.call-done = f32[2,512,400]{2,0,1:T(2,128)} async-done(((f32[2,32,400]{2,0,1:T(2,128)}), f32[2,512,400]{2,0,1:T(2,128)}) %all-gather.17.cloned.1.call-update) | async-done | bytes 1638416 | tf_op jit(solution)/shard_map/all_gather | solution.py:119
  577.8 5.0 fusion.145
  582.8 4.9 gather_fusion.6
  587.7 2.9 copy.287
  595.6 3.8 select_reduce_fusion.4
  600.2 4.2 fusion.42
  604.3 4.4 fusion.88
  608.7 3.5 gather_fusion.8
  624.5 18.1 %all-gather.3 = f32[8,2,32]{2,1,0:T(2,128)S(1)} all-gather(f32[1,2,32]{2,1,0:T(2,128)S(1)} %get-tuple-element.114), channel_id=1, replica_groups=mesh['bucket'=8,'dom'=16] {'bucket'}, dimensions={0}, use_global_device_ids=true | all-gather | bytes 2304 | tf_op jit(solution)/shard_map/all_gather | solution.py:99
  642.7 15.1 %all-gather.4 = f32[8,2,32]{2,1,0:T(2,128)S(1)} all-gather(f32[1,2,32]{2,1,0:T(2,128)S(1)} %bitcast.197), channel_id=1, replica_groups=mesh['bucket'=8,'dom'=16] {'bucket'}, dimensions={0}, use_global_device_ids=true | all-gather | bytes 2304 | tf_op jit(solution)/shard_map/all_gather | solution.py:88
  657.9 35.3 %reduce-scatter.17.cloned.1.call-done = f32[32,800]{1,0:T(8,128)} async-done(((f32[512,800]{1,0:T(8,128)}), f32[32,800]{1,0:T(8,128)}) %reduce-scatter.17.cloned.1.call-update) | async-done | bytes 102416 | tf_op jit(solution)/shard_map/reduce_scatter | solution.py:138
  694.4 32.9 %all_gather.73 = f32[16,32,400]{2,1,0:T(8,128)S(1)} all-gather(f32[2,32,400]{2,1,0:T(8,128)S(1)} %divide_subtract_fusion.1), channel_id=1, replica_groups=mesh['bucket'=8,'dom'=16] {'bucket'}, dimensions={0}, use_global_device_ids=true | all-gather | bytes 921600 | tf_op jit(solution)/shard_map/all_gather | solution.py:98
  727.5 32.1 %all_gather.74 = f32[16,32,400]{2,1,0:T(8,128)S(1)} all-gather(f32[2,32,400]{2,1,0:T(8,128)S(1)} %select_reduce_fusion.3), channel_id=1, replica_groups=mesh['bucket'=8,'dom'=16] {'bucket'}, dimensions={0}, use_global_device_ids=true | all-gather | bytes 921600 | tf_op jit(solution)/shard_map/all_gather | solution.py:87
  766.0 10.8 %gather_fusion.10 = f32[1024,400]{1,0:T(8,128)} fusion(f32[7424,400]{1,0:T(8,128)} %copy.266, s32[1024]{0:T(1024)S(1)} %fusion.114), kind=kCustom, calls=%fused_computation.11.clone | custom fusion | bytes 3280896 | tf_op jit(solution)/shard_map/jit(_take)/gather | solution.py:45
  782.4 25.0 %all-gather.19.cloned.1.call-done = f32[2,512,400]{2,0,1:T(2,128)} async-done(((f32[2,32,400]{2,0,1:T(2,128)}), f32[2,512,400]{2,0,1:T(2,128)}) %all-gather.19.cloned.1.call-update) | async-done | bytes 1638416 | tf_op jit(solution)/shard_map/all_gather | solution.py:119
  807.4 5.0 fusion.144
  812.5 4.9 gather_fusion.9
  817.4 3.0 copy.298
  825.3 3.8 select_reduce_fusion.1
  829.9 4.2 fusion.40
  834.1 4.4 fusion.85
  838.4 3.5 gather_fusion.11
  854.0 18.1 %all-gather.5 = f32[8,2,32]{2,1,0:T(2,128)S(1)} all-gather(f32[1,2,32]{2,1,0:T(2,128)S(1)} %get-tuple-element.112), channel_id=1, replica_groups=mesh['bucket'=8,'dom'=16] {'bucket'}, dimensions={0}, use_global_device_ids=true | all-gather | bytes 2304 | tf_op jit(solution)/shard_map/all_gather | solution.py:99
  872.1 15.1 %all-gather.6 = f32[8,2,32]{2,1,0:T(2,128)S(1)} all-gather(f32[1,2,32]{2,1,0:T(2,128)S(1)} %bitcast.198), channel_id=1, replica_groups=mesh['bucket'=8,'dom'=16] {'bucket'}, dimensions={0}, use_global_device_ids=true | all-gather | bytes 2304 | tf_op jit(solution)/shard_map/all_gather | solution.py:88
  887.3 35.4 %reduce-scatter.19.cloned.1.call-done = f32[32,800]{1,0:T(8,128)} async-done(((f32[512,800]{1,0:T(8,128)}), f32[32,800]{1,0:T(8,128)}) %reduce-scatter.19.cloned.1.call-update) | async-done | bytes 102416 | tf_op jit(solution)/shard_map/reduce_scatter | solution.py:138
  923.9 32.9 %all_gather.78 = f32[16,32,400]{2,1,0:T(8,128)S(1)} all-gather(f32[2,32,400]{2,1,0:T(8,128)S(1)} %divide_subtract_fusion), channel_id=1, replica_groups=mesh['bucket'=8,'dom'=16] {'bucket'}, dimensions={0}, use_global_device_ids=true | all-gather | bytes 921600 | tf_op jit(solution)/shard_map/all_gather | solution.py:98
  956.8 17.9 %all-gather.7 = f32[8,2,32]{2,1,0:T(2,128)S(1)} all-gather(f32[1,2,32]{2,1,0:T(2,128)S(1)} %get-tuple-element.110), channel_id=1, replica_groups=mesh['bucket'=8,'dom'=16] {'bucket'}, dimensions={0}, use_global_device_ids=true | all-gather | bytes 2304 | tf_op jit(solution)/shard_map/all_gather | solution.py:99
  (307 shorter events, 120.1 us)
Async XLA Ops:
  7.2 38.0 %copy-start.49 = (s32[1,128,4]{1,2,0:T(4,128)S(1)}, s32[1,128,4]{1,2,0:T(4,128)}, u32[]{:S(2)}) copy-start(s32[1,128,4]{1,2,0:T(4,128)} %param.16) | copy-start | bytes 6148
  7.2 47.5 %copy-start.31 = (s32[4,1,1,16,512]{4,3,2,1,0:T(8,128)S(1)}, s32[4,1,1,16,512]{4,3,2,1,0:T(8,128)}, u32[]{:S(2)}) copy-start(s32[4,1,1,16,512]{4,3,2,1,0:T(8,128)} %param.17) | copy-start | bytes 393220
  7.2 53.4 %copy-start.33 = (s32[1,128,4,8,3]{1,3,4,2,0:T(8,128)S(1)}, s32[1,128,4,8,3]{1,3,4,2,0:T(8,128)}, u32[]{:S(2)}) copy-start(s32[1,128,4,8,3]{1,3,4,2,0:T(8,128)} %param.15) | copy-start | bytes 147460
  7.2 113.8 %all-gather.13.cloned.1.call-start = ((), (), s32[]{:S(2)}) async-start(), calls=%async_computation.6 | async-start | bytes 2228224 | tf_op jit(solution)/shard_map/all_gather | solution.py:119
  44.1 1.8 copy-start.45
  45.9 33.4 %all-to-all-start.1 = ((s32[128,1,4]{2,1,0:T(1,128)}), s32[128,1,4]{2,1,0:T(1,128)S(1)}, u32[]{:S(2)}, u32[]{:S(2)}) async-start(s32[128,1,4]{2,1,0:T(1,128)} %bitcast.3), calls=%async_computation.1 | async-start | bytes 131072 | tf_op jit(solution)/shard_map/all_to_all | solution.py:111
  79.3 25.7 %all-to-all-start = ((s32[128,4,8,3]{2,1,3,0:T(4,128)}), s32[128,4,8,3]{2,1,3,0:T(4,128)S(1)}, u32[]{:S(2)}, u32[]{:S(2)}) async-start(s32[128,4,8,3]{2,1,3,0:T(4,128)} %bitcast), calls=%async_computation | async-start | bytes 1572864 | tf_op jit(solution)/shard_map/all_to_all | solution.py:110
  89.0 144.2 %reduce-scatter.13.cloned.1.call-start = ((), (), s32[]{:S(2)}) async-start(), calls=%async_computation.10 | async-start | bytes 1949696 | tf_op jit(solution)/shard_map/reduce_scatter | solution.py:138
  89.3 17.2 %copy-start.35 = (s32[128]{0:T(128)}, s32[128]{0:T(128)S(1)}, u32[]{:S(2)}) copy-start(s32[128]{0:T(128)S(1)} %get-tuple-element.6) | copy-start | bytes 1540
  133.9 1.9 copy-start.1
  135.8 1.9 copy-start
  135.8 2.4 copy-start.12
  159.2 1.4 copy-start.16
  160.6 1.1 copy-start.54
  161.0 2.5 copy-start.20
  161.0 2.5 copy-start.21
  165.4 1.8 copy-start.34
  165.4 2.5 copy-start.50
  165.5 17.8 %copy-start.46 = (pred[2,16]{1,0:T(4,128)(4,1)S(1)}, pred[2,16]{1,0:T(4,128)(4,1)}, u32[]{:S(2)}) copy-start(pred[2,16]{1,0:T(4,128)(4,1)} %copy-done.45) | copy-start | bytes 100
  165.5 17.9 %copy-start.53 = (s32[2]{0:T(128)S(1)}, s32[2]{0:T(128)}, u32[]{:S(2)}) copy-start(s32[2]{0:T(128)} %get-tuple-element.104) | copy-start | bytes 28
  167.2 180.8 %all-gather.15.cloned.1.call-start = ((), (), s32[]{:S(2)}) async-start(), calls=%async_computation.7 | async-start | bytes 2228224 | tf_op jit(solution)/shard_map/all_gather | solution.py:119
  183.4 116.8 %copy-start.47 = (pred[2,16]{1,0:T(4,128)(4,1)}, pred[2,16]{1,0:T(4,128)(4,1)S(1)}, u32[]{:S(2)}) copy-start(pred[2,16]{1,0:T(4,128)(4,1)S(1)} %iota_compare_fusion.33) | copy-start | bytes 100
  184.0 116.1 %copy-start.39 = (pred[2,16]{1,0:T(4,128)(4,1)}, pred[2,16]{1,0:T(4,128)(4,1)S(1)}, u32[]{:S(2)}) copy-start(pred[2,16]{1,0:T(4,128)(4,1)S(1)} %get-tuple-element.129) | copy-start | bytes 100
  301.2 162.2 %reduce-scatter.15.cloned.1.call-start = ((), (), s32[]{:S(2)}) async-start(), calls=%async_computation.11 | async-start | bytes 1949696 | tf_op jit(solution)/shard_map/reduce_scatter | solution.py:138
  304.1 2.0 copy-start.36
  304.1 2.3 copy-start.30
  361.1 1.7 copy-start.13
  362.9 1.4 copy-start.2
  364.3 1.8 copy-start.8
  386.2 1.4 copy-start.3
  386.2 1.9 copy-start.17
  388.5 2.4 copy-start.22
  388.6 2.4 copy-start.23
  392.9 1.8 copy-start.52
  392.9 1.9 copy-start.42
  392.9 19.9 %copy-start.40 = (pred[2,16]{1,0:T(4,128)(4,1)S(1)}, pred[2,16]{1,0:T(4,128)(4,1)}, u32[]{:S(2)}) copy-start(pred[2,16]{1,0:T(4,128)(4,1)} %copy-done.39) | copy-start | bytes 100
  392.9 35.1 %copy-start.48 = (pred[2,16]{1,0:T(4,128)(4,1)S(1)}, pred[2,16]{1,0:T(4,128)(4,1)}, u32[]{:S(2)}) copy-start(pred[2,16]{1,0:T(4,128)(4,1)} %copy-done.47) | copy-start | bytes 100
  394.6 102.9 %copy-start.38 = (pred[2,16]{1,0:T(4,128)(4,1)S(1)}, pred[2,16]{1,0:T(4,128)(4,1)}, u32[]{:S(2)}) copy-start(pred[2,16]{1,0:T(4,128)(4,1)} %get-tuple-element.128) | copy-start | bytes 100
  394.6 183.1 %all-gather.17.cloned.1.call-start = ((), (), s32[]{:S(2)}) async-start(), calls=%async_computation.8 | async-start | bytes 2228224 | tf_op jit(solution)/shard_map/all_gather | solution.py:119
  497.5 33.2 %copy-start.43 = (s32[1,1,2]{1,2,0:T(2,128)S(1)}, s32[1,1,2]{1,2,0:T(2,128)}, u32[]{:S(2)}) copy-start(s32[1,1,2]{1,2,0:T(2,128)} %get-tuple-element.11) | copy-start | bytes 28
  497.5 33.2 %copy-start.44 = (s32[1,1,2]{1,2,0:T(2,128)S(1)}, s32[1,1,2]{1,2,0:T(2,128)}, u32[]{:S(2)}) copy-start(s32[1,1,2]{1,2,0:T(2,128)} %get-tuple-element.107) | copy-start | bytes 28
  497.5 35.1 %copy-start.32 = (s32[16,512]{1,0:T(8,128)S(1)}, s32[16,512]{1,0:T(8,128)}, u32[]{:S(2)}) copy-start(s32[16,512]{1,0:T(8,128)} %get-tuple-element.79) | copy-start | bytes 98308
  530.7 162.5 %reduce-scatter.17.cloned.1.call-start = ((), (), s32[]{:S(2)}) async-start(), calls=%async_computation.12 | async-start | bytes 1949696 | tf_op jit(solution)/shard_map/reduce_scatter | solution.py:138
  538.9 2.4 copy-start.29
  590.7 1.7 copy-start.14
  592.4 1.4 copy-start.4
  593.8 1.8 copy-start.9
  615.9 1.4 copy-start.5
  615.9 1.9 copy-start.18
  617.8 1.1 copy-start.56
  618.3 2.4 copy-start.24
  618.3 2.4 copy-start.25
  622.6 1.8 copy-start.51
  624.3 103.0 %copy-start.37 = (pred[2,16]{1,0:T(4,128)(4,1)S(1)}, pred[2,16]{1,0:T(4,128)(4,1)}, u32[]{:S(2)}) copy-start(pred[2,16]{1,0:T(4,128)(4,1)} %get-tuple-element.127) | copy-start | bytes 100
  624.4 183.1 %all-gather.19.cloned.1.call-start = ((), (), s32[]{:S(2)}) async-start(), calls=%async_computation.9 | async-start | bytes 2228224 | tf_op jit(solution)/shard_map/all_gather | solution.py:119
  760.7 162.0 %reduce-scatter.19.cloned.1.call-start = ((), (), s32[]{:S(2)}) async-start(), calls=%async_computation.13 | async-start | bytes 1949696 | tf_op jit(solution)/shard_map/reduce_scatter | solution.py:138
  763.6 2.2 copy-start.28
  820.3 1.7 copy-start.15
  822.1 1.4 copy-start.6
  823.5 1.8 copy-start.10
  845.5 1.4 copy-start.7
  845.5 1.9 copy-start.19
  847.9 2.4 copy-start.26
  847.9 2.4 copy-start.27
  (4 other events, 4.0 us)
Sparse Core Ops, SparseCore 0:
  45.2 49.2 all-gather.12
  167.3 65.8 reduce-scatter.12
  301.3 46.6 all-gather.14
  394.8 68.5 reduce-scatter.14
  530.8 46.9 all-gather.16
  624.5 68.6 reduce-scatter.16
  760.8 46.5 all-gather.18
  854.1 68.5 reduce-scatter.18
where the time goes:
time: 992 us; the launch traced here: 983 us
  blocking collectives  395 us (40%)
  waiting for transfers between devices  240 us (24%)
  local copies, waits for them, and re-layouts  196 us (20%)
  matrix products  63.5 us (6%)
  other arithmetic  49 us (5%)
  between operations  20.7 us (2%)
  starting transfers between devices  18.9 us (2%)
    reduce_scatter x4, waiting for transfers between devices, local(): lax.psum_scatter(jnp.concatenate([src_side, dst_side], axis=1), 'dom', sc...  155 us
    all_gather x4, blocking collectives, send_home(): lax.all_gather(rows_held, 'bucket', axis=0, tiled=True)  132 us
    all_gather x4, blocking collectives, fetch_rows(): lax.all_gather(rows_held, 'bucket', axis=0, tiled=True)  131 us
    all_gather x4, blocking collectives, send_home(): lax.all_gather(state_held, 'bucket', axis=0, tiled=True)  72.1 us
    all_gather x4, waiting for transfers between devices, local(): full_rows = lax.all_gather(mine_rows, 'dom', axis=1, tiled=True)  70 us
    all_gather x4, blocking collectives, fetch_rows(): lax.all_gather(state_held, 'bucket', axis=0, tiled=True)  60.6 us
    gather x8, local copies, waits for them, and re-layouts, slot_terms(): rel_rows = jnp.take(relations, triples[:, 1], axis=0)  51.5 us
    unnamed x129, local copies, waits for them, and re-layouts  42.7 us
  transfers between devices with their start and end apart: 10, of which 8 were waited for; matrix products, arithmetic and copies ran while one was open for 11% of the time, Pallas kernels for 0%

commit v1 on v0

--- a/solution.py
+++ b/solution.py
@@ -84,7 +84,10 @@
         labels_all,
         wanted,
         (
-            lax.all_gather(rows_held, "bucket", axis=0, tiled=True),
+            jnp.concatenate(
+                lax.all_to_all(jnp.stack([rows_held] * lax.axis_size("bucket")), "bucket", 0, 0),
+                axis=0,
+            ),
             lax.all_gather(state_held, "bucket", axis=0, tiled=True),
         ),
     )

time: 992 us -> 929 us (0.936)
  blocking collectives: 395 us -> 264 us
  waiting for transfers between devices: 240 us -> 286 us
  starting transfers between devices: 18.9 us -> 35.8 us
    all_gather x4 -> x0, blocking collectives: 131 us -> none  [fetch_rows(): lax.all_gather(rows_held, 'bucket', axis=0, tiled=True)]
    all_to_all x0 -> x4, waiting for transfers between devices: none -> 47.2 us  [fetch_rows(): lax.all_to_all(jnp.stack([rows_held] * lax.axis_size('bucket')), 'bucket'...]
    all_to_all x0 -> x4, starting transfers between devices: none -> 18.6 us  [fetch_rows(): lax.all_to_all(jnp.stack([rows_held] * lax.axis_size('bucket')), 'bucket'...]
    unnamed x129 -> x125, local copies, waits for them, and re-layouts: 42.7 us -> 42.7 us
  transfers between devices with their start and end apart: 10 -> 14, of which waited for: 8 -> 12; matrix products, arithmetic and copies ran while one was open for 11% -> 12% of each run, Pallas kernels for 0% -> 0%
where the time goes in v1:
time: 929 us; the launch traced here: 920 us
  waiting for transfers between devices  286 us (31%)
  blocking collectives  264 us (28%)
  local copies, waits for them, and re-layouts  201 us (22%)
  matrix products  63.5 us (7%)
  other arithmetic  49.2 us (5%)
  starting transfers between devices  35.8 us (4%)
  between operations  20.7 us (2%)
    reduce_scatter x4, waiting for transfers between devices, local(): lax.psum_scatter(jnp.concatenate([src_side, dst_side], axis=1), 'dom', sc...  156 us
    all_gather x4, blocking collectives, send_home(): lax.all_gather(rows_held, 'bucket', axis=0, tiled=True)  131 us
    all_gather x4, blocking collectives, send_home(): lax.all_gather(state_held, 'bucket', axis=0, tiled=True)  72.1 us
    all_gather x4, waiting for transfers between devices, local(): full_rows = lax.all_gather(mine_rows, 'dom', axis=1, tiled=True)  66.6 us
    all_gather x4, blocking collectives, fetch_rows(): lax.all_gather(state_held, 'bucket', axis=0, tiled=True)  60.5 us
    gather x8, local copies, waits for them, and re-layouts, slot_terms(): rel_rows = jnp.take(relations, triples[:, 1], axis=0)  51.6 us
    all_to_all x4, waiting for transfers between devices, fetch_rows(): lax.all_to_all(jnp.stack([rows_held] * lax.axis_size('bucket')), 'bucket'...  47.2 us
    unnamed x125, local copies, waits for them, and re-layouts  42.7 us
  transfers between devices with their start and end apart: 14, of which 12 were waited for; matrix products, arithmetic and copies ran while one was open for 12% of the time, Pallas kernels for 0%

profile of v1, /device:TPU:2, one launch (start us, length us, event | category | flops | bytes accessed | tf_op | source)
XLA Modules:
  0.0 920.1 jit_solution(6599666799235193215)
XLA Ops:
  9.2 6.5 all-to-all-start
  18.4 12.9 %all-to-all-done = f32[8,2,32,400]{3,2,1,0:T(8,128)S(1)} async-done(((f32[8,2,32,400]{3,2,1,0:T(8,128)}), f32[8,2,32,400]{3,2,1,0:T(8,128)S(1)}, u32[]{:S(2)}, u32[]{:S(2)}) %all-to-all-start) | async-done | bytes 819232 | tf_op jit(solution)/shard_map/all_to_all | solution.py:88
  31.4 7.1 all-to-all-start.2
  39.5 4.7 convert_reduce_fusion.2
  47.3 14.2 %copy.266 = f32[7424,400]{1,0:T(8,128)} copy(f32[7424,400]{0,1:T(8,128)} %param.13) | data formatting | bytes 23756800 | tf_op args[2]
  63.5 9.8 %all-to-all-start.1 = ((s32[128,4,8,3]{2,1,3,0:T(4,128)}), s32[128,4,8,3]{2,1,3,0:T(4,128)S(1)}, u32[]{:S(2)}, u32[]{:S(2)}) async-start(s32[128,4,8,3]{2,1,3,0:T(4,128)} %bitcast.1), calls=%async_computation.1 | async-start | bytes 1572864 | tf_op jit(solution)/shard_map/all_to_all | solution.py:113
  75.1 15.7 %all-to-all-done.1 = s32[128,4,8,3]{2,1,3,0:T(4,128)S(1)} async-done(((s32[128,4,8,3]{2,1,3,0:T(4,128)}), s32[128,4,8,3]{2,1,3,0:T(4,128)S(1)}, u32[]{:S(2)}, u32[]{:S(2)}) %all-to-all-start.1) | async-done | bytes 49184 | tf_op jit(solution)/shard_map/all_to_all | solution.py:113
  92.4 9.5 %gather_fusion.1 = f32[1024,400]{1,0:T(8,128)S(1)} fusion(f32[7424,400]{1,0:T(8,128)} %copy.266, s32[1024]{0:T(1024)S(1)} %fusion.105), kind=kCustom, calls=%fused_computation.1.clone | custom fusion | bytes 3280896 | tf_op jit(solution)/shard_map/jit(_take)/gather | solution.py:45
  107.1 4.0 fusion.147
  112.1 4.9 gather_fusion
  124.3 3.8 select_reduce_fusion.10
  129.0 4.2 fusion.46
  133.1 4.4 fusion.94
  137.5 4.9 gather_fusion.2
  153.9 15.2 %all-gather = f32[8,2,32]{2,1,0:T(2,128)S(1)} all-gather(f32[1,2,32]{2,1,0:T(2,128)S(1)} %bitcast.207), channel_id=1, replica_groups=mesh['bucket'=8,'dom'=16] {'bucket'}, dimensions={0}, use_global_device_ids=true | all-gather | bytes 2304 | tf_op jit(solution)/shard_map/all_gather | solution.py:91
  169.8 50.1 %reduce-scatter.13.cloned.1.call-done = f32[32,800]{1,0:T(8,128)} async-done(((f32[512,800]{1,0:T(8,128)}), f32[32,800]{1,0:T(8,128)}) %reduce-scatter.13.cloned.1.call-update) | async-done | bytes 102416 | tf_op jit(solution)/shard_map/reduce_scatter | solution.py:141
  221.7 32.8 %all_gather.50 = f32[16,32,400]{2,1,0:T(8,128)S(1)} all-gather(f32[2,32,400]{2,1,0:T(8,128)S(1)} %divide_subtract_fusion.3), channel_id=1, replica_groups=mesh['bucket'=8,'dom'=16] {'bucket'}, dimensions={0}, use_global_device_ids=true | all-gather | bytes 921600 | tf_op jit(solution)/shard_map/all_gather | solution.py:101
  255.8 4.2 all-to-all-start.3
  260.1 11.4 %all-to-all-done.3 = f32[8,2,32,400]{3,2,1,0:T(8,128)S(1)} async-done(((f32[8,2,32,400]{3,2,1,0:T(8,128)}), f32[8,2,32,400]{3,2,1,0:T(8,128)S(1)}, u32[]{:S(2)}, u32[]{:S(2)}) %all-to-all-start.3) | async-done | bytes 819232 | tf_op jit(solution)/shard_map/all_to_all | solution.py:88
  277.9 10.7 %gather_fusion.4 = f32[1024,400]{1,0:T(8,128)} fusion(f32[7424,400]{1,0:T(8,128)} %copy.266, s32[1024]{0:T(1024)S(1)} %fusion.108), kind=kCustom, calls=%fused_computation.9.clone | custom fusion | bytes 3280896 | tf_op jit(solution)/shard_map/jit(_take)/gather | solution.py:45
  294.3 23.7 %all-gather.15.cloned.1.call-done = f32[2,512,400]{2,0,1:T(2,128)} async-done(((f32[2,32,400]{2,0,1:T(2,128)}), f32[2,512,400]{2,0,1:T(2,128)}) %all-gather.15.cloned.1.call-update) | async-done | bytes 1638416 | tf_op jit(solution)/shard_map/all_gather | solution.py:122
  318.1 5.0 fusion.146
  323.1 4.9 gather_fusion.3
  328.0 3.1 copy.276
  336.1 3.8 select_reduce_fusion.7
  340.7 4.2 fusion.44
  344.9 4.4 fusion.91
  349.3 3.5 gather_fusion.5
  364.7 18.1 %all-gather.1 = f32[8,2,32]{2,1,0:T(2,128)S(1)} all-gather(f32[1,2,32]{2,1,0:T(2,128)S(1)} %copy-done.42), channel_id=1, replica_groups=mesh['bucket'=8,'dom'=16] {'bucket'}, dimensions={0}, use_global_device_ids=true | all-gather | bytes 2304 | tf_op jit(solution)/shard_map/all_gather | solution.py:102
  382.9 15.1 %all-gather.2 = f32[8,2,32]{2,1,0:T(2,128)S(1)} all-gather(f32[1,2,32]{2,1,0:T(2,128)S(1)} %bitcast.204), channel_id=1, replica_groups=mesh['bucket'=8,'dom'=16] {'bucket'}, dimensions={0}, use_global_device_ids=true | all-gather | bytes 2304 | tf_op jit(solution)/shard_map/all_gather | solution.py:91
  398.1 35.4 %reduce-scatter.15.cloned.1.call-done = f32[32,800]{1,0:T(8,128)} async-done(((f32[512,800]{1,0:T(8,128)}), f32[32,800]{1,0:T(8,128)}) %reduce-scatter.15.cloned.1.call-update) | async-done | bytes 102416 | tf_op jit(solution)/shard_map/reduce_scatter | solution.py:141
  434.6 32.7 %all_gather.54 = f32[16,32,400]{2,1,0:T(8,128)S(1)} all-gather(f32[2,32,400]{2,1,0:T(8,128)S(1)} %divide_subtract_fusion.2), channel_id=1, replica_groups=mesh['bucket'=8,'dom'=16] {'bucket'}, dimensions={0}, use_global_device_ids=true | all-gather | bytes 921600 | tf_op jit(solution)/shard_map/all_gather | solution.py:101
  468.7 4.1 all-to-all-start.4
  472.9 11.4 %all-to-all-done.4 = f32[8,2,32,400]{3,2,1,0:T(8,128)S(1)} async-done(((f32[8,2,32,400]{3,2,1,0:T(8,128)}), f32[8,2,32,400]{3,2,1,0:T(8,128)S(1)}, u32[]{:S(2)}, u32[]{:S(2)}) %all-to-all-start.4) | async-done | bytes 819232 | tf_op jit(solution)/shard_map/all_to_all | solution.py:88
  487.4 4.7 convert_reduce_fusion
  496.3 10.6 %gather_fusion.7 = f32[1024,400]{1,0:T(8,128)} fusion(f32[7424,400]{1,0:T(8,128)} %copy.266, s32[1024]{0:T(1024)S(1)} %fusion.111), kind=kCustom, calls=%fused_computation.10.clone | custom fusion | bytes 3280896 | tf_op jit(solution)/shard_map/jit(_take)/gather | solution.py:45
  512.5 18.6 %all-gather.17.cloned.1.call-done = f32[2,512,400]{2,0,1:T(2,128)} async-done(((f32[2,32,400]{2,0,1:T(2,128)}), f32[2,512,400]{2,0,1:T(2,128)}) %all-gather.17.cloned.1.call-update) | async-done | bytes 1638416 | tf_op jit(solution)/shard_map/all_gather | solution.py:122
  531.2 5.0 fusion.145
  536.2 4.9 gather_fusion.6
  541.1 2.9 copy.287
  549.0 3.8 select_reduce_fusion.4
  553.6 4.2 fusion.42
  557.8 4.4 fusion.88
  562.1 3.5 gather_fusion.8
  577.8 18.1 %all-gather.3 = f32[8,2,32]{2,1,0:T(2,128)S(1)} all-gather(f32[1,2,32]{2,1,0:T(2,128)S(1)} %get-tuple-element.114), channel_id=1, replica_groups=mesh['bucket'=8,'dom'=16] {'bucket'}, dimensions={0}, use_global_device_ids=true | all-gather | bytes 2304 | tf_op jit(solution)/shard_map/all_gather | solution.py:102
  595.9 15.1 %all-gather.4 = f32[8,2,32]{2,1,0:T(2,128)S(1)} all-gather(f32[1,2,32]{2,1,0:T(2,128)S(1)} %bitcast.205), channel_id=1, replica_groups=mesh['bucket'=8,'dom'=16] {'bucket'}, dimensions={0}, use_global_device_ids=true | all-gather | bytes 2304 | tf_op jit(solution)/shard_map/all_gather | solution.py:91
  611.2 35.4 %reduce-scatter.17.cloned.1.call-done = f32[32,800]{1,0:T(8,128)} async-done(((f32[512,800]{1,0:T(8,128)}), f32[32,800]{1,0:T(8,128)}) %reduce-scatter.17.cloned.1.call-update) | async-done | bytes 102416 | tf_op jit(solution)/shard_map/reduce_scatter | solution.py:141
  647.8 32.7 %all_gather.58 = f32[16,32,400]{2,1,0:T(8,128)S(1)} all-gather(f32[2,32,400]{2,1,0:T(8,128)S(1)} %divide_subtract_fusion.1), channel_id=1, replica_groups=mesh['bucket'=8,'dom'=16] {'bucket'}, dimensions={0}, use_global_device_ids=true | all-gather | bytes 921600 | tf_op jit(solution)/shard_map/all_gather | solution.py:101
  681.8 3.9 all-to-all-start.5
  685.8 11.4 %all-to-all-done.5 = f32[8,2,32,400]{3,2,1,0:T(8,128)S(1)} async-done(((f32[8,2,32,400]{3,2,1,0:T(8,128)}), f32[8,2,32,400]{3,2,1,0:T(8,128)S(1)}, u32[]{:S(2)}, u32[]{:S(2)}) %all-to-all-start.5) | async-done | bytes 819232 | tf_op jit(solution)/shard_map/all_to_all | solution.py:88
  703.6 10.7 %gather_fusion.10 = f32[1024,400]{1,0:T(8,128)} fusion(f32[7424,400]{1,0:T(8,128)} %copy.266, s32[1024]{0:T(1024)S(1)} %fusion.114), kind=kCustom, calls=%fused_computation.11.clone | custom fusion | bytes 3280896 | tf_op jit(solution)/shard_map/jit(_take)/gather | solution.py:45
  719.9 24.2 %all-gather.19.cloned.1.call-done = f32[2,512,400]{2,0,1:T(2,128)} async-done(((f32[2,32,400]{2,0,1:T(2,128)}), f32[2,512,400]{2,0,1:T(2,128)}) %all-gather.19.cloned.1.call-update) | async-done | bytes 1638416 | tf_op jit(solution)/shard_map/all_gather | solution.py:122
  744.2 5.0 fusion.144
  749.3 4.9 gather_fusion.9
  754.2 2.9 copy.298
  762.1 3.8 select_reduce_fusion.1
  766.6 4.2 fusion.40
  770.8 4.4 fusion.85
  775.2 3.5 gather_fusion.11
  790.7 18.1 %all-gather.5 = f32[8,2,32]{2,1,0:T(2,128)S(1)} all-gather(f32[1,2,32]{2,1,0:T(2,128)S(1)} %get-tuple-element.112), channel_id=1, replica_groups=mesh['bucket'=8,'dom'=16] {'bucket'}, dimensions={0}, use_global_device_ids=true | all-gather | bytes 2304 | tf_op jit(solution)/shard_map/all_gather | solution.py:102
  808.9 15.1 %all-gather.6 = f32[8,2,32]{2,1,0:T(2,128)S(1)} all-gather(f32[1,2,32]{2,1,0:T(2,128)S(1)} %bitcast.206), channel_id=1, replica_groups=mesh['bucket'=8,'dom'=16] {'bucket'}, dimensions={0}, use_global_device_ids=true | all-gather | bytes 2304 | tf_op jit(solution)/shard_map/all_gather | solution.py:91
  824.1 35.4 %reduce-scatter.19.cloned.1.call-done = f32[32,800]{1,0:T(8,128)} async-done(((f32[512,800]{1,0:T(8,128)}), f32[32,800]{1,0:T(8,128)}) %reduce-scatter.19.cloned.1.call-update) | async-done | bytes 102416 | tf_op jit(solution)/shard_map/reduce_scatter | solution.py:141
  860.7 32.9 %all_gather.62 = f32[16,32,400]{2,1,0:T(8,128)S(1)} all-gather(f32[2,32,400]{2,1,0:T(8,128)S(1)} %divide_subtract_fusion), channel_id=1, replica_groups=mesh['bucket'=8,'dom'=16] {'bucket'}, dimensions={0}, use_global_device_ids=true | all-gather | bytes 921600 | tf_op jit(solution)/shard_map/all_gather | solution.py:101
  893.6 17.9 %all-gather.7 = f32[8,2,32]{2,1,0:T(2,128)S(1)} all-gather(f32[1,2,32]{2,1,0:T(2,128)S(1)} %get-tuple-element.110), channel_id=1, replica_groups=mesh['bucket'=8,'dom'=16] {'bucket'}, dimensions={0}, use_global_device_ids=true | all-gather | bytes 2304 | tf_op jit(solution)/shard_map/all_gather | solution.py:102
  (311 shorter events, 136.8 us)
Async XLA Ops:
  7.2 8.5 copy-start.47
  7.2 9.2 %copy-start.34 = (s32[4,8,2]{1,2,0:T(2,128)S(1)}, s32[4,8,2]{1,2,0:T(2,128)}, u32[]{:S(2)}) copy-start(s32[4,8,2]{1,2,0:T(2,128)} %param.14) | copy-start | bytes 772
  7.2 10.6 %copy-start.31 = (s32[4,1,1,16,512]{4,3,2,1,0:T(8,128)S(1)}, s32[4,1,1,16,512]{4,3,2,1,0:T(8,128)}, u32[]{:S(2)}) copy-start(s32[4,1,1,16,512]{4,3,2,1,0:T(8,128)} %param.17) | copy-start | bytes 393220
  9.2 35.6 %copy-start.33 = (s32[1,128,4,8,3]{1,3,4,2,0:T(8,128)S(1)}, s32[1,128,4,8,3]{1,3,4,2,0:T(8,128)}, u32[]{:S(2)}) copy-start(s32[1,128,4,8,3]{1,3,4,2,0:T(8,128)} %param.15) | copy-start | bytes 147460
  9.2 22.2 %all-to-all-start = ((f32[8,2,32,400]{3,2,1,0:T(8,128)}), f32[8,2,32,400]{3,2,1,0:T(8,128)S(1)}, u32[]{:S(2)}, u32[]{:S(2)}) async-start(f32[8,2,32,400]{3,2,1,0:T(8,128)} %stack.32), calls=%async_computation | async-start | bytes 2097152 | tf_op jit(solution)/shard_map/all_to_all | solution.py:88
  17.8 21.7 %copy-start.45 = (pred[2,16]{1,0:T(4,128)(4,1)}, pred[2,16]{1,0:T(4,128)(4,1)S(1)}, u32[]{:S(2)}) copy-start(pred[2,16]{1,0:T(4,128)(4,1)S(1)} %iota_compare_fusion.32) | copy-start | bytes 100
  31.4 32.2 %all-to-all-start.2 = ((s32[128,1,4]{2,1,0:T(1,128)}), s32[128,1,4]{2,1,0:T(1,128)S(1)}, u32[]{:S(2)}, u32[]{:S(2)}) async-start(s32[128,1,4]{2,1,0:T(1,128)} %bitcast.4), calls=%async_computation.2 | async-start | bytes 131072 | tf_op jit(solution)/shard_map/all_to_all | solution.py:114
  38.4 68.7 %all-gather.13.cloned.1.call-start = ((), (), s32[]{:S(2)}) async-start(), calls=%async_computation.10 | async-start | bytes 2228224 | tf_op jit(solution)/shard_map/all_gather | solution.py:122
  63.5 27.3 %all-to-all-start.1 = ((s32[128,4,8,3]{2,1,3,0:T(4,128)}), s32[128,4,8,3]{2,1,3,0:T(4,128)S(1)}, u32[]{:S(2)}, u32[]{:S(2)}) async-start(s32[128,4,8,3]{2,1,3,0:T(4,128)} %bitcast.1), calls=%async_computation.1 | async-start | bytes 1572864 | tf_op jit(solution)/shard_map/all_to_all | solution.py:113
  73.3 146.6 %reduce-scatter.13.cloned.1.call-start = ((), (), s32[]{:S(2)}) async-start(), calls=%async_computation.14 | async-start | bytes 1949696 | tf_op jit(solution)/shard_map/reduce_scatter | solution.py:141
  74.2 18.2 %copy-start.36 = (s32[128]{0:T(128)}, s32[128]{0:T(128)S(1)}, u32[]{:S(2)}) copy-start(s32[128]{0:T(128)S(1)} %get-tuple-element.6) | copy-start | bytes 1540
  119.9 1.9 copy-start.1
  121.9 1.9 copy-start
  121.9 2.4 copy-start.12
  145.3 1.4 copy-start.16
  147.0 2.5 copy-start.20
  147.0 2.5 copy-start.21
  151.5 2.4 copy-start.48
  151.5 17.6 %copy-start.46 = (pred[2,16]{1,0:T(4,128)(4,1)S(1)}, pred[2,16]{1,0:T(4,128)(4,1)}, u32[]{:S(2)}) copy-start(pred[2,16]{1,0:T(4,128)(4,1)} %copy-done.45) | copy-start | bytes 100
  169.8 86.0 %copy-start.39 = (pred[2,16]{1,0:T(4,128)(4,1)}, pred[2,16]{1,0:T(4,128)(4,1)S(1)}, u32[]{:S(2)}) copy-start(pred[2,16]{1,0:T(4,128)(4,1)S(1)} %get-tuple-element.129) | copy-start | bytes 100
  254.5 5.6 copy-start.51
  255.8 15.7 %all-to-all-start.3 = ((f32[8,2,32,400]{3,2,1,0:T(8,128)}), f32[8,2,32,400]{3,2,1,0:T(8,128)S(1)}, u32[]{:S(2)}, u32[]{:S(2)}) async-start(f32[8,2,32,400]{3,2,1,0:T(8,128)} %stack.36), calls=%async_computation.3 | async-start | bytes 2097152 | tf_op jit(solution)/shard_map/all_to_all | solution.py:88
  260.0 58.1 %all-gather.15.cloned.1.call-start = ((), (), s32[]{:S(2)}) async-start(), calls=%async_computation.11 | async-start | bytes 2228224 | tf_op jit(solution)/shard_map/all_gather | solution.py:122
  272.6 160.9 %reduce-scatter.15.cloned.1.call-start = ((), (), s32[]{:S(2)}) async-start(), calls=%async_computation.15 | async-start | bytes 1949696 | tf_op jit(solution)/shard_map/reduce_scatter | solution.py:141
  275.5 2.0 copy-start.37
  275.5 2.3 copy-start.30
  331.2 1.7 copy-start.13
  332.9 1.4 copy-start.2
  334.3 1.8 copy-start.8
  356.2 1.4 copy-start.3
  356.3 1.9 copy-start.17
  358.6 2.4 copy-start.22
  358.6 2.4 copy-start.23
  363.0 1.7 copy-start.42
  363.0 19.8 %copy-start.40 = (pred[2,16]{1,0:T(4,128)(4,1)S(1)}, pred[2,16]{1,0:T(4,128)(4,1)}, u32[]{:S(2)}) copy-start(pred[2,16]{1,0:T(4,128)(4,1)} %copy-done.39) | copy-start | bytes 100
  364.7 102.7 %copy-start.38 = (pred[2,16]{1,0:T(4,128)(4,1)S(1)}, pred[2,16]{1,0:T(4,128)(4,1)}, u32[]{:S(2)}) copy-start(pred[2,16]{1,0:T(4,128)(4,1)} %get-tuple-element.128) | copy-start | bytes 100
  467.3 5.5 copy-start.50
  468.7 16.7 %copy-start.43 = (s32[1,1,2]{1,2,0:T(2,128)S(1)}, s32[1,1,2]{1,2,0:T(2,128)}, u32[]{:S(2)}) copy-start(s32[1,1,2]{1,2,0:T(2,128)} %get-tuple-element.11) | copy-start | bytes 28
  468.7 16.7 %copy-start.44 = (s32[1,1,2]{1,2,0:T(2,128)S(1)}, s32[1,1,2]{1,2,0:T(2,128)}, u32[]{:S(2)}) copy-start(s32[1,1,2]{1,2,0:T(2,128)} %get-tuple-element.107) | copy-start | bytes 28
  468.7 18.7 %copy-start.32 = (s32[16,512]{1,0:T(8,128)S(1)}, s32[16,512]{1,0:T(8,128)}, u32[]{:S(2)}) copy-start(s32[16,512]{1,0:T(8,128)} %get-tuple-element.79) | copy-start | bytes 98308
  468.7 15.7 %all-to-all-start.4 = ((f32[8,2,32,400]{3,2,1,0:T(8,128)}), f32[8,2,32,400]{3,2,1,0:T(8,128)S(1)}, u32[]{:S(2)}, u32[]{:S(2)}) async-start(f32[8,2,32,400]{3,2,1,0:T(8,128)} %stack.40), calls=%async_computation.4 | async-start | bytes 2097152 | tf_op jit(solution)/shard_map/all_to_all | solution.py:88
  472.8 58.3 %all-gather.17.cloned.1.call-start = ((), (), s32[]{:S(2)}) async-start(), calls=%async_computation.12 | async-start | bytes 2228224 | tf_op jit(solution)/shard_map/all_gather | solution.py:122
  485.4 161.2 %reduce-scatter.17.cloned.1.call-start = ((), (), s32[]{:S(2)}) async-start(), calls=%async_computation.16 | async-start | bytes 1949696 | tf_op jit(solution)/shard_map/reduce_scatter | solution.py:141
  493.7 2.0 copy-start.35
  493.7 2.4 copy-start.29
  544.1 1.7 copy-start.14
  545.8 1.4 copy-start.4
  547.2 1.8 copy-start.9
  569.4 1.4 copy-start.5
  569.4 1.9 copy-start.18
  571.8 2.4 copy-start.24
  571.8 2.4 copy-start.25
  680.5 5.3 copy-start.49
  681.8 15.4 %all-to-all-start.5 = ((f32[8,2,32,400]{3,2,1,0:T(8,128)}), f32[8,2,32,400]{3,2,1,0:T(8,128)S(1)}, u32[]{:S(2)}, u32[]{:S(2)}) async-start(f32[8,2,32,400]{3,2,1,0:T(8,128)} %stack.44), calls=%async_computation.5 | async-start | bytes 2097152 | tf_op jit(solution)/shard_map/all_to_all | solution.py:88
  685.7 58.5 %all-gather.19.cloned.1.call-start = ((), (), s32[]{:S(2)}) async-start(), calls=%async_computation.13 | async-start | bytes 2228224 | tf_op jit(solution)/shard_map/all_gather | solution.py:122
  698.2 161.3 %reduce-scatter.19.cloned.1.call-start = ((), (), s32[]{:S(2)}) async-start(), calls=%async_computation.17 | async-start | bytes 1949696 | tf_op jit(solution)/shard_map/reduce_scatter | solution.py:141
  701.1 2.2 copy-start.28
  757.1 1.7 copy-start.15
  758.9 1.4 copy-start.6
  760.3 1.8 copy-start.10
  782.3 1.4 copy-start.7
  782.3 1.9 copy-start.19
  784.7 2.4 copy-start.26
  784.7 2.4 copy-start.27
  (6 other events, 6.2 us)
Sparse Core Ops, SparseCore 0:
  42.3 57.4 all-gather.12
  153.3 66.5 reduce-scatter.12
  272.7 45.3 all-gather.14
  364.8 68.5 reduce-scatter.14
  485.5 45.6 all-gather.16
  577.9 68.6 reduce-scatter.16
  698.3 45.7 all-gather.18
  790.9 68.6 reduce-scatter.18
